TPU v7x, 32 devices: a whole 2x2x4 slice. The times are simulated.
32 devices in a mesh: expert: 16 (over z, y, x), tensor: 2 (over core).
Axes of the slice: x: 2, y: 2, z: 4, core: 2. Of those that a mesh axis runs over, the one named last changes fastest.
Arguments:
- tokens: bfloat16 [256, 3584], P('expert', 'tensor'), may hold values from -6 to 6
- grad_out: bfloat16 [256, 3584], P('expert', 'tensor'), may hold values from -6 to 6
- gate_weights: bfloat16 [256, 8], P('expert'), may hold values from 0.099609375 to 1
- routing: int32 [256, 8], P('expert'), may hold values from 0 to 15, all different within a row; in each aligned block of 16 rows (0 to 15, 16 to 31, ...) at most 12 rows name the same one
- w_gate: bfloat16 [16, 3584, 1024], P('expert', None, 'tensor'), may hold values from -0.09375 to 0.09375
- w_up: bfloat16 [16, 3584, 1024], P('expert', None, 'tensor'), may hold values from -0.09375 to 0.09375
- w_down: bfloat16 [16, 1024, 3584], P('expert', 'tensor'), may hold values from -0.1875 to 0.1875
Outputs:
- grad_tokens: bfloat16 [256, 3584], P('expert', 'tensor')
- grad_gate: bfloat16 [16, 3584, 1024], P('expert', None, 'tensor')
- grad_up: bfloat16 [16, 3584, 1024], P('expert', None, 'tensor')
Inputs may be any that keep to these rules, and one draw needn't show every extreme that they name: `routing`: each row names 8 different experts; within the rows of one device (aligned blocks of 16 rows) no expert is named by more than 12 rows.
All inputs are finite; a program needn't handle non-finite values.
Results may differ from a plain program's by a relative error of at most 0.014.
Values may be sent and summed in bfloat16 or wider, within the bound.
A program may use at most 64 MiB of HBM per device.

v0:
```python
import jax
import jax.numpy as jnp
from jax import lax
from jax.sharding import PartitionSpec as P


def contract_first(left, right):
    return lax.dot_general(
        left, right, (((0,), (0,)), ((), ())), preferred_element_type=jnp.float32
    )


def contract_last(left, right):
    return lax.dot_general(
        left, right, (((1,), (1,)), ((), ())), preferred_element_type=jnp.float32
    )


def body(tokens, grad_out, gate_weights, routing, w_gate, w_up, w_down):
    experts = lax.axis_size("expert")
    tok_rows = routing.shape[0]
    picks_each = routing.shape[1]
    width = w_gate.shape[1]
    capacity = 3 * tok_rows * picks_each // (2 * experts)
    slot_count = experts * capacity
    picks = routing.reshape(-1)
    table = (picks[:, None] == jnp.arange(experts, dtype=jnp.int32)[None, :]).astype(jnp.int32)
    before = jnp.cumsum(table, axis=0) - table
    place = jnp.sum(before * table, axis=1)
    slot_of = picks * capacity + place
    owner = jnp.arange(tok_rows * picks_each, dtype=jnp.int32) // picks_each
    source_row = jnp.zeros((slot_count,), jnp.int32).at[slot_of].set(owner)
    slot_gate = jnp.zeros((slot_count,), jnp.bfloat16).at[slot_of].set(gate_weights.reshape(-1))
    part_w = tokens.shape[1]
    send_x = tokens[source_row].reshape(experts, capacity, part_w)
    send_dy = grad_out[source_row].reshape(experts, capacity, part_w)
    part_x, part_dy, got_gate = (
        lax.all_to_all(send_x, "expert", split_axis=0, concat_axis=0, tiled=True),
        lax.all_to_all(send_dy, "expert", split_axis=0, concat_axis=0, tiled=True),
        lax.all_to_all(
            slot_gate.reshape(experts, capacity), "expert", split_axis=0, concat_axis=0, tiled=True
        ),
    )
    got_x, got_dy = (
        lax.all_gather(part_x, "tensor", axis=2, tiled=True),
        lax.all_gather(part_dy, "tensor", axis=2, tiled=True),
    )
    rows_x = got_x.reshape(slot_count, width)
    rows_dy = got_dy.reshape(slot_count, width)
    scale = got_gate.reshape(slot_count).astype(jnp.float32)
    weight_g = w_gate[0]
    weight_u = w_up[0]
    weight_d = w_down[0]
    pre_gate = jnp.dot(rows_x, weight_g, preferred_element_type=jnp.float32)
    pre_up = jnp.dot(rows_x, weight_u, preferred_element_type=jnp.float32)
    back_act = contract_last(rows_dy, weight_d)
    sig = jax.nn.sigmoid(pre_gate)
    d_gate = (scale[:, None] * back_act * pre_up * sig * (1.0 + pre_gate * (1.0 - sig))).astype(
        jnp.bfloat16
    )
    d_up = (scale[:, None] * back_act * pre_gate * sig).astype(jnp.bfloat16)
    grad_g = contract_first(rows_x, d_gate).astype(jnp.bfloat16)[None]
    grad_u = contract_first(rows_x, d_up).astype(jnp.bfloat16)[None]
    partial_value = contract_last(d_gate, weight_g) + contract_last(d_up, weight_u)
    rounded = partial_value.astype(jnp.bfloat16)
    shares = lax.psum_scatter(
        rounded.astype(jnp.float32).astype(jnp.bfloat16), "tensor", scatter_dimension=1, tiled=True
    ).astype(jnp.float32)
    returned = lax.all_to_all(
        shares.reshape(experts, capacity, shares.shape[1]).astype(jnp.bfloat16),
        "expert",
        split_axis=0,
        concat_axis=0,
        tiled=True,
    ).astype(jnp.float32)
    flat_back = returned.reshape(slot_count, shares.shape[1])
    result = jnp.sum(flat_back[slot_of].reshape(tok_rows, picks_each, shares.shape[1]), axis=1)
    grad_tokens = result.astype(jnp.bfloat16)
    return (grad_tokens, grad_g, grad_u)


def solution(mesh):
    placed = (
        P("expert", "tensor"),
        P("expert", "tensor"),
        P("expert", None),
        P("expert", None),
        P("expert", None, "tensor"),
        P("expert", None, "tensor"),
        P("expert", "tensor", None),
    )
    return jax.shard_map(
        body,
        mesh=mesh,
        in_specs=placed,
        out_specs=(P("expert", "tensor"), P("expert", None, "tensor"), P("expert", None, "tensor")),
        check_vma=False,
    )
```

profile of v0, /device:TPU:0, one launch (start us, length us, event | category | flops | bytes accessed | tf_op | source)
XLA Modules:
  0.0 146.6 jit_solution(17413520131053665552)
XLA Ops:
  7.9 0.8 copy.17
  9.4 1.0 scatter_custom_fusion.1
  10.4 1.1 gather_fusion.1
  11.7 32.0 %all_to_all.25 = bf16[16,12,1792]{2,1,0:T(8,128)(2,1)} all-to-all(bf16[16,12,1792]{2,1,0:T(8,128)(2,1)S(1)} %reshape.78), channel_id=1, replica_groups=mesh['expert'=16,'tensor'=2] {'expert'}, dimensions={0} | all-to-all | bytes 1376256 | tf_op jit(solution)/shard_map/all_to_all | solution.py:38
  43.9 1.1 gather_fusion
  45.2 26.6 %all_to_all.26 = bf16[16,12,1792]{2,1,0:T(8,128)(2,1)} all-to-all(bf16[16,12,1792]{2,1,0:T(8,128)(2,1)S(1)} %reshape.76), channel_id=1, replica_groups=mesh['expert'=16,'tensor'=2] {'expert'}, dimensions={0} | all-to-all | bytes 1376256 | tf_op jit(solution)/shard_map/all_to_all | solution.py:39
  72.1 1.3 scatter_custom_fusion
  73.5 10.7 %all_to_all.27 = bf16[16,1,12]{2,1,0:T(2,128)(2,1)S(1)} all-to-all(bf16[16,1,12]{2,1,0:T(2,128)(2,1)S(1)} %all_to_all.20), channel_id=1, replica_groups=mesh['expert'=16,'tensor'=2] {'expert'}, dimensions={0} | all-to-all | bytes 768 | tf_op jit(solution)/shard_map/all_to_all | solution.py:40
  84.4 2.4 %reshape.79 = bf16[192,3584]{1,0:T(8,128)(2,1)S(1)} reshape(bf16[16,12,3584]{2,1,0:T(8,128)(2,1)} %all-gather.5.cloned.1.call-done) | data formatting | bytes 2752512 | tf_op jit(solution)/shard_map/reshape | solution.py:48
  86.7 2.9 %fusion.5 = f32[192,512]{1,0:T(8,128)S(1)} fusion(bf16[192,3584]{1,0:T(8,128)(2,1)S(1)} %reshape.79, bf16[1,3584,512]{2,1,0:T(8,128)(2,1)} %param.11), kind=kOutput, calls=%fused_computation.13 | convolution fusion | flops 704643072 | bytes 5439488 | tf_op jit(solution)/shard_map/dot_general | solution.py:54
  89.7 2.4 %reshape.77 = bf16[192,3584]{1,0:T(8,128)(2,1)S(1)} reshape(bf16[16,12,3584]{2,1,0:T(8,128)(2,1)} %all-gather.3.cloned.1.call-done) | data formatting | bytes 2752512 | tf_op jit(solution)/shard_map/reshape | solution.py:49
  92.1 3.5 %multiply_convert_fusion = (bf16[192,512]{1,0:T(8,128)(2,1)S(1)}, f32[192,512]{1,0:T(8,128)S(1)}) fusion(f32[192,512]{1,0:T(8,128)S(1)} %fusion.5, bf16[192,3584]{1,0:T(8,128)(2,1)S(1)} %reshape.77, bf16[1,512,3584]{2,1,0:T(8,128)(2,1)} %param.13, f32[192]{0:T(256)S(1)} %reshape.83), kind=kOutput, calls=%fused_computation.26 | convolution fusion | flops 705331200 | bytes 6030080 | tf_op jit(solution)/shard_map/dot_general | solution.py:14
  95.7 0.9 fusion.24
  96.6 1.1 copy-done.2
  97.7 1.4 fusion.3
  99.0 2.4 %fusion.2 = bf16[192,3584]{1,0:T(8,128)(2,1)} fusion(f32[192,3584]{1,0:T(8,128)S(1)} %fusion.3, bf16[192,512]{1,0:T(8,128)(2,1)S(1)} %get-tuple-element.3, bf16[1,3584,512]{2,1,0:T(8,128)(2,1)S(1)} %copy-done.3), kind=kOutput, calls=%fused_computation.10 | convolution fusion | flops 706019328 | bytes 7995392 | tf_op jit(solution)/shard_map/dot_general | solution.py:14
  101.5 5.4 %reduce-scatter.2.cloned.1.call-done = bf16[192,1792]{1,0:T(8,128)(2,1)} async-done(((bf16[192,3584]{1,0:T(8,128)(2,1)}), bf16[192,1792]{1,0:T(8,128)(2,1)}) %reduce-scatter.2.cloned.1.call-update) | async-done | bytes 688144 | tf_op jit(solution)/shard_map/reduce_scatter | solution.py:66
  106.9 2.1 %convert_element_type.45 = bf16[16,12,1792]{2,1,0:T(8,128)(2,1)} reshape(bf16[192,1792]{1,0:T(8,128)(2,1)} %reduce-scatter.2.cloned.1.call-done) | data formatting | bytes 1376256 | tf_op jit(solution)/shard_map/convert_element_type | solution.py:70
  109.0 6.8 %all-to-all-start.3 = ((bf16[16,12,1792]{2,1,0:T(8,128)(2,1)}), bf16[16,12,1792]{2,1,0:T(8,128)(2,1)S(1)}, u32[]{:S(2)}, u32[]{:S(2)}) async-start(bf16[16,12,1792]{2,1,0:T(8,128)(2,1)} %convert_element_type.45), calls=%async_computation.4 | async-start | bytes 1835008 | tf_op jit(solution)/shard_map/all_to_all | solution.py:69
  115.8 3.0 %fusion.1 = bf16[1,3584,512]{2,1,0:T(8,128)(2,1)} fusion(bf16[192,3584]{1,0:T(8,128)(2,1)S(1)} %reshape.79, bf16[192,512]{1,0:T(8,128)(2,1)S(1)} %get-tuple-element.3), kind=kOutput, calls=%fused_computation.8 | convolution fusion | flops 706478080 | bytes 5242880 | tf_op jit(solution)/shard_map/dot_general | solution.py:8
  118.8 3.0 %fusion = bf16[1,3584,512]{2,1,0:T(8,128)(2,1)} fusion(bf16[192,3584]{1,0:T(8,128)(2,1)S(1)} %reshape.79, bf16[192,512]{1,0:T(8,128)(2,1)S(1)} %fusion.24), kind=kOutput, calls=%fused_computation.7 | convolution fusion | flops 706478080 | bytes 5242880 | tf_op jit(solution)/shard_map/dot_general | solution.py:8
  121.8 16.3 %all-to-all-done.3 = bf16[16,12,1792]{2,1,0:T(8,128)(2,1)S(1)} async-done(((bf16[16,12,1792]{2,1,0:T(8,128)(2,1)}), bf16[16,12,1792]{2,1,0:T(8,128)(2,1)S(1)}, u32[]{:S(2)}, u32[]{:S(2)}) %all-to-all-start.3) | async-done | bytes 688160 | tf_op jit(solution)/shard_map/all_to_all | solution.py:69
  138.3 1.0 gather_fusion.2
  139.3 0.9 bitcast_reduce_fusion
  (37 shorter events, 2.5 us)
Async XLA Ops:
  7.2 3.2 %copy-start = (bf16[16,1792]{1,0:T(8,128)(2,1)S(1)}, bf16[16,1792]{1,0:T(8,128)(2,1)}, u32[]{:S(2)}) copy-start(bf16[16,1792]{1,0:T(8,128)(2,1)} %param.7) | copy-start | bytes 172036
  7.2 77.2 %all-gather.5.cloned.1.call-start = ((), (), s32[]{:S(2)}) async-start(), calls=%async_computation.6 | async-start | bytes 2752512 | tf_op jit(solution)/shard_map/all_gather | solution.py:45
  11.6 32.3 %copy-start.1 = (bf16[16,1792]{1,0:T(8,128)(2,1)S(1)}, bf16[16,1792]{1,0:T(8,128)(2,1)}, u32[]{:S(2)}) copy-start(bf16[16,1792]{1,0:T(8,128)(2,1)} %param.8) | copy-start | bytes 172036
  43.8 45.9 %all-gather.3.cloned.1.call-start = ((), (), s32[]{:S(2)}) async-start(), calls=%async_computation.5 | async-start | bytes 2752512 | tf_op jit(solution)/shard_map/all_gather | solution.py:46
  45.0 26.9 %copy-start.4 = (bf16[16,8]{0,1:T(8,128)(2,1)S(1)}, bf16[16,8]{0,1:T(8,128)(2,1)}, u32[]{:S(2)}) copy-start(bf16[16,8]{0,1:T(8,128)(2,1)} %param.9) | copy-start | bytes 772
  71.8 35.0 %reduce-scatter.2.cloned.1.call-start = ((), (), s32[]{:S(2)}) async-start(), calls=%async_computation.7 | async-start | bytes 2064384 | tf_op jit(solution)/shard_map/reduce_scatter | solution.py:66
  92.1 3.6 %copy-start.3 = (bf16[1,3584,512]{2,1,0:T(8,128)(2,1)S(1)}, bf16[1,3584,512]{2,1,0:T(8,128)(2,1)}, u32[]{:S(2)}) copy-start(bf16[1,3584,512]{2,1,0:T(8,128)(2,1)} %param.12) | copy-start | bytes 11010052
  95.6 2.0 %copy-start.2 = (bf16[1,3584,512]{2,1,0:T(8,128)(2,1)S(1)}, bf16[1,3584,512]{2,1,0:T(8,128)(2,1)}, u32[]{:S(2)}) copy-start(bf16[1,3584,512]{2,1,0:T(8,128)(2,1)} %param.11) | copy-start | bytes 11010052
  109.0 29.2 %all-to-all-start.3 = ((bf16[16,12,1792]{2,1,0:T(8,128)(2,1)}), bf16[16,12,1792]{2,1,0:T(8,128)(2,1)S(1)}, u32[]{:S(2)}, u32[]{:S(2)}) async-start(bf16[16,12,1792]{2,1,0:T(8,128)(2,1)} %convert_element_type.45), calls=%async_computation.4 | async-start | bytes 1835008 | tf_op jit(solution)/shard_map/all_to_all | solution.py:69
Sparse Core Ops, SparseCore 0:
  43.9 8.1 all-gather.4
  72.0 8.1 all-gather.2
  101.6 5.2 reduce-scatter.1
where the time goes:
time: 147 us
  blocking collectives  69.4 us (47%)
  waiting for transfers between devices  21.8 us (15%)
  matrix products  17.2 us (12%)
  local copies, waits for them, and re-layouts  15.3 us (10%)
  between operations  14 us (10%)
  starting transfers between devices  6.94 us (5%)
  other arithmetic  2.03 us (1%)
    all_to_all x1, blocking collectives, body(): lax.all_to_all(send_x, 'expert', split_axis=0, concat_axis=0, tiled=True)  32 us
    all_to_all x1, blocking collectives, body(): lax.all_to_all(send_dy, 'expert', split_axis=0, concat_axis=0, tiled=True)  26.6 us
    all_to_all x1, waiting for transfers between devices, body(): lax.all_to_all(shares.reshape(experts, capacity, shares.shape[1]).astype(...  16.3 us
    all_to_all x1, blocking collectives, body(): lax.all_to_all(slot_gate.reshape(experts, capacity), 'expert', split_axis...  10.7 us
    dot_general x3, matrix products, contract_last(): lax.dot_general(left, right, (((1,), (1,)), ((), ())), preferred_element_...  7.34 us
    all_to_all x1, starting transfers between devices, body(): lax.all_to_all(shares.reshape(experts, capacity, shares.shape[1]).astype(...  6.81 us
    dot_general x2, matrix products, contract_first(): lax.dot_general(left, right, (((0,), (0,)), ((), ())), preferred_element_...  6 us
    reduce_scatter x1, waiting for transfers between devices, body(): lax.psum_scatter(rounded.astype(jnp.float32).astype(jnp.bfloat16), 'tenso...  5.38 us
  transfers between devices with their start and end apart: 4, of which 2 were waited for; matrix products, arithmetic and copies ran while one was open for 10% of the time, Pallas kernels for 0%

commit v1 on v0

v1 whole, which is shorter than its diff:
```python
import functools
import jax
import jax.numpy as jnp
from jax import lax
from jax.experimental import pallas as pl
from jax.experimental.pallas import tpu as pltpu
from jax.sharding import PartitionSpec as P

LANES = 128
TILE = 256


def contract_first(left, right):
    return lax.dot_general(
        left, right, (((0,), (0,)), ((), ())), preferred_element_type=jnp.float32
    )


def contract_last(left, right):
    return lax.dot_general(
        left, right, (((1,), (1,)), ((), ())), preferred_element_type=jnp.float32
    )


def act_grads(scale, back_act, pre_gate, pre_up):
    sig = jax.nn.sigmoid(pre_gate)
    d_gate = scale * back_act * pre_up * sig * (1.0 + pre_gate * (1.0 - sig))
    d_up = scale * back_act * pre_gate * sig
    return d_gate.astype(jnp.bfloat16), d_up.astype(jnp.bfloat16)


def kernel(
    tok, gro, gw, rt, wg_hbm, wu_hbm, wd_hbm,
    gt_out, x_out, dg, du,
    x_buf, dy_buf, wg, wu, wd, pre_g, pre_u, part_out, part_in, acc, r2, r1, rz,
    w_sem, xo_sem, z_s, z_r, p1_s, p1_r, p2_s, p2_r, pe_s, pe_r,
    rpe_s, rpe_r, r2_s, r2_r, r1_s, r1_r, rz_s, rz_r,
):
    e = lax.axis_index("expert")
    c = lax.axis_index("tensor")
    rows, half = tok.shape
    total = x_buf.shape[1]
    hidden = wg.shape[1]
    z, y, x = e // 4, (e // 2) % 2, e % 2
    flip_y, flip_x = 2 * (1 - 2 * y), 1 - 2 * x
    flip1 = (1 - c) * flip_y + c * flip_x
    flip2 = (1 - c) * flip_x + c * flip_y
    other1 = c * flip_y + (1 - c) * flip_x
    other2 = c * flip_x + (1 - c) * flip_y
    peer = (e, 1 - c)
    part1 = (e + flip1, c)
    part2 = (e + flip2, c)

    def column(k):
        return lax.rem(z + k, 4) * 4 + 2 * y + x

    def at(owner):
        return pl.ds(pl.multiple_of(owner * rows, 16), rows)

    weights = [
        pltpu.make_async_copy(src, dst, w_sem.at[i])
        for i, (src, dst) in enumerate(((wg_hbm, wg), (wu_hbm, wu), (wd_hbm, wd)))
    ]
    for copy in weights:
        copy.start()

    barrier = pltpu.get_barrier_semaphore()
    for device in [(column(k), c) for k in (1, 2, 3)] + [part1, part2, peer]:
        pl.semaphore_signal(barrier, inc=1, device_id=device, device_id_type=pl.DeviceIdType.MESH)

    picks = rt[...]
    gates = gw[...].astype(jnp.float32)
    lane = lax.broadcasted_iota(jnp.int32, (rows, LANES), 1)
    table = jnp.zeros((rows, LANES), jnp.float32)
    for k in range(picks.shape[1]):
        table += jnp.where(lane == picks[:, k : k + 1], gates[:, k : k + 1], 0.0)
    x_buf[c, at(e), 0:half] = tok[...]
    x_buf[c, at(e), half : half + LANES] = table.astype(jnp.bfloat16)
    dy_buf[c, at(e), :] = gro[...]
    pl.semaphore_wait(barrier, 6)

    bufs = (x_buf, dy_buf)
    sent = []

    def remote(src, dst, send_sem, recv_sem, device):
        return pltpu.make_async_remote_copy(
            src_ref=src, dst_ref=dst, send_sem=send_sem, recv_sem=recv_sem,
            device_id=device, device_id_type=pl.DeviceIdType.MESH,
        )

    def chunk_copy(kind, owner, core, sems, idx, device):
        ref = bufs[kind].at[core, at(owner), :]
        return remote(ref, ref, sems[0].at[kind, idx], sems[1].at[kind, idx], device)

    def go(copy):
        copy.start()
        sent.append(copy)

    zs, p1, p2, pe = (z_s, z_r), (p1_s, p1_r), (p2_s, p2_r), (pe_s, pe_r)

    def to_peer(kind, k, a, b):
        owner = column(k) + a * flip1 + b * flip2
        go(chunk_copy(kind, owner, c, pe, k * 4 + a * 2 + b, peer))

    def to_part2(kind, k, a):
        go(chunk_copy(kind, column(k) + a * flip1, c, p2, k * 2 + a, part2))

    def to_part1(kind, k):
        go(chunk_copy(kind, column(k), c, p1, k, part1))

    def own(kind):
        for k in (2, 1, 3):
            go(chunk_copy(kind, e, c, zs, k - 1, (column(k), c)))
        to_part1(kind, 0)
        to_part2(kind, 0, 0)
        to_peer(kind, 0, 0, 0)

    def from_column(kind, k):
        chunk_copy(kind, column(k), c, zs, 3 - k, (column(k), c)).wait_recv()
        to_part1(kind, k)
        to_part2(kind, k, 0)
        to_peer(kind, k, 0, 0)

    def from_part1(kind, k):
        chunk_copy(kind, column(k) + flip1, c, p1, k, part1).wait_recv()
        to_part2(kind, k, 1)
        to_peer(kind, k, 1, 0)

    def from_part2(kind, k, a):
        owner = column(k) + a * flip1 + flip2
        chunk_copy(kind, owner, c, p2, k * 2 + a, part2).wait_recv()
        to_peer(kind, k, a, 1)

    def from_peer(kind):
        for k in range(4):
            for a in range(2):
                for b in range(2):
                    owner = column(k) + a * other1 + b * other2
                    chunk_copy(kind, owner, 1 - c, pe, k * 4 + a * 2 + b, peer).wait_recv()

    def pre(weight, out, n):
        cols = pl.ds(n * TILE, TILE)
        out[:, cols] = jnp.dot(
            x_buf[0, :, 0:half], weight[0:half, cols], preferred_element_type=jnp.float32
        ) + jnp.dot(
            x_buf[1, :, 0:half], weight[half : 2 * half, cols], preferred_element_type=jnp.float32
        )

    own(0)
    from_part1(0, 0)
    from_column(0, 1)
    from_column(0, 3)
    from_part2(0, 0, 0)
    from_column(0, 2)
    own(1)
    from_part1(0, 1)
    from_part2(0, 0, 1)
    from_part1(0, 3)
    from_part1(0, 2)
    from_part2(0, 1, 0)
    from_part1(1, 0)
    from_part2(0, 1, 1)
    from_column(1, 1)
    from_part2(0, 3, 0)
    from_column(1, 3)
    from_part2(0, 3, 1)
    from_part2(0, 2, 0)
    from_part2(0, 2, 1)
    from_column(1, 2)
    from_part2(1, 0, 0)
    from_peer(0)
    x_copies = [
        pltpu.make_async_copy(
            x_buf.at[h, :, 0:half], x_out.at[:, h * half : (h + 1) * half], xo_sem.at[h]
        )
        for h in range(2)
    ]
    for copy in x_copies:
        copy.start()
    work = [(weight, out, n) for weight, out in ((wg, pre_g), (wu, pre_u)) for n in range(hidden // TILE)]
    rest = [
        functools.partial(from_part1, 1, 1),
        functools.partial(from_part2, 1, 0, 1),
        functools.partial(from_part1, 1, 3),
        functools.partial(from_part1, 1, 2),
        functools.partial(from_part2, 1, 1, 0),
        functools.partial(from_part2, 1, 1, 1),
        functools.partial(from_part2, 1, 3, 0),
        functools.partial(from_part2, 1, 3, 1),
        functools.partial(from_part2, 1, 2, 0),
        functools.partial(from_part2, 1, 2, 1),
    ]
    weights[0].wait()
    weights[1].wait()
    for i, event in enumerate(rest):
        event()
        if 0 < i <= len(work):
            pre(*work[i - 1])
    for item in work[len(rest) - 1 :]:
        pre(*item)
    lanes = lax.broadcasted_iota(jnp.int32, (total, LANES), 1)
    scale = jnp.sum(
        jnp.where(lanes == e, x_buf[0, :, half : half + LANES].astype(jnp.float32), 0.0),
        axis=1, keepdims=True,
    )
    weights[2].wait()
    from_peer(1)
    for n in range(hidden // TILE):
        cols = pl.ds(n * TILE, TILE)
        back = contract_last(dy_buf[0], wd[cols, 0:half]) + contract_last(
            dy_buf[1], wd[cols, half : 2 * half]
        )
        one, two = act_grads(scale, back, pre_g[:, cols], pre_u[:, cols])
        dg[:, cols] = one
        du[:, cols] = two

    def partial(core, n):
        place = pl.ds(pl.multiple_of(core * half + n * TILE, TILE), TILE)
        return contract_last(dg[...], wg[place, :]) + contract_last(du[...], wu[place, :])

    tiles = half // TILE
    for n in range(tiles):
        cols = pl.ds(n * TILE, TILE)
        part_out[:, cols] = partial(1 - c, n).astype(jnp.bfloat16)
        go(remote(part_out.at[:, cols], part_in.at[:, cols], rpe_s.at[n], rpe_r.at[n], peer))
    for n in range(tiles):
        cols = pl.ds(n * TILE, TILE)
        mine = partial(c, n)
        remote(part_out.at[:, cols], part_in.at[:, cols], rpe_s.at[n], rpe_r.at[n], peer).wait_recv()
        acc[:, cols] = (mine + part_in[:, cols].astype(jnp.float32)).astype(jnp.bfloat16)

    def add(owner, ref):
        acc[at(owner), :] = (
            acc[at(owner), :].astype(jnp.float32) + ref[...].astype(jnp.float32)
        ).astype(jnp.bfloat16)

    order = (2, 1, 3, 0)

    def second(k, a, owner):
        idx = k * 2 + a
        return remote(acc.at[at(owner), :], r2.at[idx], r2_s.at[idx], r2_r.at[idx], part2)

    def first(k, owner):
        return remote(acc.at[at(owner), :], r1.at[k], r1_s.at[k], r1_r.at[k], part1)

    def third(k, device):
        return remote(acc.at[at(column(k)), :], rz.at[k - 1], rz_s.at[k - 1], rz_r.at[k - 1], device)

    for k in order:
        for a in (1, 0):
            go(second(k, a, column(k) + a * flip1 + flip2))
    for k in order:
        for a in (1, 0):
            second(k, a, column(k) + a * flip1 + flip2).wait_recv()
            add(column(k) + a * flip1, r2.at[k * 2 + a])
            if a == 1:
                go(first(k, column(k) + flip1))
    for k in order:
        first(k, column(k) + flip1).wait_recv()
        add(column(k), r1.at[k])
        if k:
            go(third(k, (column(k), c)))
    result = acc[at(e), :].astype(jnp.float32)
    for k in (1, 2, 3):
        third(k, (column(k), c)).wait_recv()
        result += rz[k - 1].astype(jnp.float32)
    gt_out[...] = result.astype(jnp.bfloat16)
    for copy in x_copies:
        copy.wait()
    for copy in sent:
        copy.wait_send()


def fused(tokens, grad_out, gate_weights, routing, w_gate, w_up, w_down):
    experts = lax.axis_size("expert")
    rows, half = tokens.shape
    total = experts * rows
    width, hidden = w_gate.shape[1:]
    vmem = pl.BlockSpec(memory_space=pltpu.VMEM)
    hbm = pl.BlockSpec(memory_space=pl.ANY)
    bf16 = jnp.bfloat16
    dma = pltpu.SemaphoreType.DMA
    tiles = half // TILE
    grad_tokens, rows_x, d_gate, d_up = pl.pallas_call(
        kernel,
        out_shape=(
            jax.ShapeDtypeStruct((rows, half), bf16),
            jax.ShapeDtypeStruct((total, width), bf16),
            jax.ShapeDtypeStruct((total, hidden), bf16),
            jax.ShapeDtypeStruct((total, hidden), bf16),
        ),
        in_specs=[vmem] * 4 + [hbm] * 3,
        out_specs=(vmem, hbm, vmem, vmem),
        scratch_shapes=[
            pltpu.VMEM((2, total, half + LANES), bf16),
            pltpu.VMEM((2, total, half), bf16),
            pltpu.VMEM((width, hidden), bf16),
            pltpu.VMEM((width, hidden), bf16),
            pltpu.VMEM((hidden, width), bf16),
            pltpu.VMEM((total, hidden), jnp.float32),
            pltpu.VMEM((total, hidden), jnp.float32),
            pltpu.VMEM((total, half), bf16),
            pltpu.VMEM((total, half), bf16),
            pltpu.VMEM((total, half), bf16),
            pltpu.VMEM((8, rows, half), bf16),
            pltpu.VMEM((4, rows, half), bf16),
            pltpu.VMEM((3, rows, half), bf16),
            dma((3,)), dma((2,)),
            dma((2, 3)), dma((2, 3)), dma((2, 4)), dma((2, 4)),
            dma((2, 8)), dma((2, 8)), dma((2, 16)), dma((2, 16)),
            dma((tiles,)), dma((tiles,)), dma((8,)), dma((8,)),
            dma((4,)), dma((4,)), dma((3,)), dma((3,)),
        ],
        compiler_params=pltpu.CompilerParams(
            collective_id=0, has_side_effects=True, vmem_limit_bytes=60 << 20
        ),
        cost_estimate=pl.CostEstimate(
            flops=10 * total * width * hidden, bytes_accessed=6 * width * hidden, transcendentals=0
        ),
        name="gather_grads_scatter",
    )(tokens, grad_out, gate_weights, routing, w_gate[0], w_up[0], w_down[0])
    grad_g = contract_first(rows_x, d_gate).astype(bf16)[None]
    grad_u = contract_first(rows_x, d_up).astype(bf16)[None]
    return (grad_tokens, grad_g, grad_u)


def dense(tokens, grad_out, gate_weights, routing, w_gate, w_up, w_down):
    me = lax.axis_index("expert")
    weight = jnp.sum(
        jnp.where(
            routing[:, None, :] == jnp.arange(lax.axis_size("expert"))[None, :, None],
            gate_weights[:, None, :],
            jnp.bfloat16(0),
        ).astype(jnp.float32),
        axis=2,
    ).astype(jnp.bfloat16)
    both = jnp.stack([tokens, grad_out])
    got = lax.all_gather(both, "expert", axis=1, tiled=True)
    got = lax.all_gather(got, "tensor", axis=2, tiled=True)
    got_weight = lax.all_gather(weight, "expert", axis=0, tiled=True)
    scale = lax.dynamic_slice_in_dim(got_weight, me, 1, axis=1).astype(jnp.float32)
    rows_x, rows_dy = got[0], got[1]
    weight_g, weight_u, weight_d = w_gate[0], w_up[0], w_down[0]
    pre_gate = jnp.dot(rows_x, weight_g, preferred_element_type=jnp.float32)
    pre_up = jnp.dot(rows_x, weight_u, preferred_element_type=jnp.float32)
    back_act = contract_last(rows_dy, weight_d)
    d_gate, d_up = act_grads(scale, back_act, pre_gate, pre_up)
    grad_g = contract_first(rows_x, d_gate).astype(jnp.bfloat16)[None]
    grad_u = contract_first(rows_x, d_up).astype(jnp.bfloat16)[None]
    part = (contract_last(d_gate, weight_g) + contract_last(d_up, weight_u)).astype(jnp.bfloat16)
    part = lax.psum_scatter(part, "tensor", scatter_dimension=1, tiled=True)
    grad_tokens = lax.psum_scatter(part, "expert", scatter_dimension=0, tiled=True)
    return (grad_tokens, grad_g, grad_u)


def solution(mesh):
    placed = (
        P("expert", "tensor"),
        P("expert", "tensor"),
        P("expert", None),
        P("expert", None),
        P("expert", None, "tensor"),
        P("expert", None, "tensor"),
        P("expert", "tensor", None),
    )
    small = mesh.shape["expert"] == 16 and mesh.shape["tensor"] == 2
    return jax.shard_map(
        fused if small else dense,
        mesh=mesh,
        in_specs=placed,
        out_specs=(P("expert", "tensor"), P("expert", None, "tensor"), P("expert", None, "tensor")),
        check_vma=False,
    )
```

time: 147 us -> 67 us (0.46)
  blocking collectives: 69.4 us -> 0 us
  Pallas kernels: 0 us -> 55.2 us
  waiting for transfers between devices: 21.8 us -> 0 us
  between operations: 14 us -> 0.66 us
  local copies, waits for them, and re-layouts: 15.3 us -> 3.34 us
  matrix products: 17.2 us -> 7.62 us
  starting transfers between devices: 6.94 us -> 0 us
  other arithmetic: 2.03 us -> 0 us
    all_to_all x3 -> x0, blocking collectives: 69.4 us -> none  [the longest x1 32 us: body(): lax.all_to_all(send_x, 'expert', split_axis=0, concat_axis=0, tiled=True)]
    pallas_call x0 -> x1, Pallas kernels: none -> 55.2 us  [fused(): pl.pallas_call(kernel, out_shape=(jax.ShapeDtypeStruct((rows, half), bf16...]
    all_to_all x1 -> x0, waiting for transfers between devices: 16.3 us -> none  [body(): lax.all_to_all(shares.reshape(experts, capacity, shares.shape[1]).astype(...]
    dot_general x5 -> x0, matrix products: 11.2 us -> none  [the longest x3 7.34 us: contract_last(): lax.dot_general(left, right, (((1,), (1,)), ((), ())), preferred_element_...]
    all_to_all x1 -> x0, starting transfers between devices: 6.81 us -> none  [body(): lax.all_to_all(shares.reshape(experts, capacity, shares.shape[1]).astype(...]
    reduce_scatter x1 -> x0, waiting for transfers between devices: 5.38 us -> none  [body(): lax.psum_scatter(rounded.astype(jnp.float32).astype(jnp.bfloat16), 'tenso...]
    reshape x6 -> x0, local copies, waits for them, and re-layouts: 5.28 us -> none  [the longest x1 2.37 us: body(): rows_x = got_x.reshape(slot_count, width)]
    gather x3 -> x0, local copies, waits for them, and re-layouts: 3.26 us -> none  [the longest x1 1.14 us: body(): send_dy = grad_out[source_row].reshape(experts, capacity, part_w)]
  transfers between devices with their start and end apart: 4 -> 0, of which waited for: 2 -> 0; matrix products, arithmetic and copies ran while one was open for 10% -> 0% of each run, Pallas kernels for 0% -> 0%
where the time goes in v1:
time: 67 us; the launch traced here: 66.8 us
  Pallas kernels  55.2 us (82%)
  matrix products  7.62 us (11%)
  local copies, waits for them, and re-layouts  3.34 us (5%)
    pallas_call x1, Pallas kernels, fused(): pl.pallas_call(kernel, out_shape=(jax.ShapeDtypeStruct((rows, half), bf16...  55.2 us
    dot_general x2, matrix products, contract_first(): lax.dot_general(left, right, (((0,), (0,)), ((), ())), preferred_element_...  7.62 us
    unnamed x9, local copies, waits for them, and re-layouts  3.34 us

profile of v1, /device:TPU:0, one launch (start us, length us, event | category | flops | bytes accessed | tf_op | source)
XLA Modules:
  0.0 66.8 jit_solution(13722706853048121934)
XLA Ops:
  0.6 1.3 %copy.10.gw = bf16[16,8]{1,0:T(8,128)(2,1)} copy(bf16[16,8]{0,1:T(8,128)(2,1)} %param.9) | data formatting | bytes 512 | tf_op args[2]
  2.0 1.4 %copy.11.rt = s32[16,8]{1,0:T(8,128)} copy(s32[16,8]{0,1:T(8,128)} %param.10) | data formatting | bytes 1024 | tf_op args[3]
  3.3 55.2 %gather_grads_scatter.1 = (bf16[16,1792]{1,0:T(8,128)(2,1)}, bf16[256,3584]{1,0:T(8,128)(2,1)}, bf16[256,512]{1,0:T(8,128)(2,1)}, bf16[256,512]{1,0:T(8,128)(2,1)}) custom-call(bf16[16,1792]{1,0:T(8,128)(2,1)} %tok.1, bf16[16,1792]{1,0:T(8,128)(2,1)} %gro.1, bf16[16,8]{1,0:T(8,128)(2,1)} %copy.10.gw, s32[16,8]{1,0:T(8,128)} %copy.11.rt, ...), custom_call_target="tpu_custom_call" | custom-call | flops 4697620480 | bytes 11010048 | tf_op jit(solution)/shard_map/gather_grads_scatter/pallas_call | solution.py:284
  58.5 0.0 copy-start
  58.5 0.0 copy-start.1
  58.5 4.6 %fusion = bf16[1,3584,512]{2,1,0:T(8,128)(2,1)} fusion(bf16[256,3584]{1,0:T(8,128)(2,1)} %get-tuple-element.8, bf16[256,512]{1,0:T(8,128)(2,1)} %get-tuple-element.9), kind=kOutput, calls=%fused_computation.2 | convolution fusion | flops 941359104 | bytes 5767168 | tf_op jit(solution)/shard_map/dot_general | solution.py:14
  63.2 0.0 copy-done
  63.2 0.0 copy-done.1
  63.2 0.0 copy-start.2
  63.2 3.0 %fusion.1 = bf16[1,3584,512]{2,1,0:T(8,128)(2,1)} fusion(bf16[256,3584]{1,0:T(8,128)(2,1)S(1)} %copy-done, bf16[256,512]{1,0:T(8,128)(2,1)S(1)} %copy-done.1), kind=kOutput, calls=%fused_computation.3 | convolution fusion | flops 941359104 | bytes 5767168 | tf_op jit(solution)/shard_map/dot_general | solution.py:14
  66.1 0.0 copy-done.2
  66.2 0.6 copy.13
Async XLA Ops:
  58.5 4.7 %copy-start = (bf16[256,3584]{1,0:T(8,128)(2,1)S(1)}, bf16[256,3584]{1,0:T(8,128)(2,1)}, u32[]{:S(2)}) copy-start(bf16[256,3584]{1,0:T(8,128)(2,1)} %get-tuple-element.8) | copy-start | bytes 5505028
  58.5 4.7 %copy-start.1 = (bf16[256,512]{1,0:T(8,128)(2,1)S(1)}, bf16[256,512]{1,0:T(8,128)(2,1)}, u32[]{:S(2)}) copy-start(bf16[256,512]{1,0:T(8,128)(2,1)} %get-tuple-element.10) | copy-start | bytes 786436
  63.2 3.0 %copy-start.2 = (bf16[16,1792]{1,0:T(8,128)(2,1)S(1)}, bf16[16,1792]{1,0:T(8,128)(2,1)}, u32[]{:S(2)}) copy-start(bf16[16,1792]{1,0:T(8,128)(2,1)} %get-tuple-element.14) | copy-start | bytes 172036

commit v2 on v1

--- a/solution.py
+++ b/solution.py
@@ -29,18 +29,25 @@
     return d_gate.astype(jnp.bfloat16), d_up.astype(jnp.bfloat16)
 
 
+def weight_grads(x_ref, d_ref, gate_ref, up_ref):
+    hidden = gate_ref.shape[2]
+    both = contract_first(x_ref[...], d_ref[...]).astype(jnp.bfloat16)
+    gate_ref[0] = both[:, 0:hidden]
+    up_ref[0] = both[:, hidden : 2 * hidden]
+
+
 def kernel(
     tok, gro, gw, rt, wg_hbm, wu_hbm, wd_hbm,
-    gt_out, x_out, dg, du,
-    x_buf, dy_buf, wg, wu, wd, pre_g, pre_u, part_out, part_in, acc, r2, r1, rz,
-    w_sem, xo_sem, z_s, z_r, p1_s, p1_r, p2_s, p2_r, pe_s, pe_r,
+    gt_out, x_out, d_all,
+    x_buf, dy_buf, wgu, wd, pre_all, back_buf, part_out, part_in, acc, r2, r1, rz,
+    in_sem, w_sem, xo_sem, z_s, z_r, p1_s, p1_r, p2_s, p2_r, pe_s, pe_r,
     rpe_s, rpe_r, r2_s, r2_r, r1_s, r1_r, rz_s, rz_r,
 ):
     e = lax.axis_index("expert")
     c = lax.axis_index("tensor")
     rows, half = tok.shape
     total = x_buf.shape[1]
-    hidden = wg.shape[1]
+    hidden = wd.shape[0]
     z, y, x = e // 4, (e // 2) % 2, e % 2
     flip_y, flip_x = 2 * (1 - 2 * y), 1 - 2 * x
     flip1 = (1 - c) * flip_y + c * flip_x
@@ -57,11 +64,26 @@
     def at(owner):
         return pl.ds(pl.multiple_of(owner * rows, 16), rows)
 
+    inputs = [
+        pltpu.make_async_copy(src, dst, in_sem.at[i])
+        for i, (src, dst) in enumerate(
+            (
+                (tok, x_buf.at[c, at(e), 0:half]),
+                (gro, dy_buf.at[c, at(e), :]),
+            )
+        )
+    ]
     weights = [
         pltpu.make_async_copy(src, dst, w_sem.at[i])
-        for i, (src, dst) in enumerate(((wg_hbm, wg), (wu_hbm, wu), (wd_hbm, wd)))
+        for i, (src, dst) in enumerate(
+            (
+                (wg_hbm, wgu.at[:, 0:hidden]),
+                (wu_hbm, wgu.at[:, hidden : 2 * hidden]),
+                (wd_hbm, wd),
+            )
+        )
     ]
-    for copy in weights:
+    for copy in inputs + weights:
         copy.start()
 
     barrier = pltpu.get_barrier_semaphore()
@@ -70,13 +92,17 @@
 
     picks = rt[...]
     gates = gw[...].astype(jnp.float32)
-    lane = lax.broadcasted_iota(jnp.int32, (rows, LANES), 1)
-    table = jnp.zeros((rows, LANES), jnp.float32)
-    for k in range(picks.shape[1]):
-        table += jnp.where(lane == picks[:, k : k + 1], gates[:, k : k + 1], 0.0)
-    x_buf[c, at(e), 0:half] = tok[...]
+    expert = lax.broadcasted_iota(jnp.int32, (LANES, rows), 0)
+    table = jnp.zeros((LANES, rows), jnp.float32)
+    for k in range(picks.shape[0]):
+        table += jnp.where(expert == picks[k : k + 1, :], gates[k : k + 1, :], 0.0)
+    row = lax.broadcasted_iota(jnp.int32, (rows, rows), 0)
+    col = lax.broadcasted_iota(jnp.int32, (rows, rows), 1)
+    eye = jnp.where(row == col, 1.0, 0.0).astype(jnp.bfloat16)
+    table = contract_last(eye, table.astype(jnp.bfloat16))
     x_buf[c, at(e), half : half + LANES] = table.astype(jnp.bfloat16)
-    dy_buf[c, at(e), :] = gro[...]
+    inputs[0].wait()
+    inputs[1].wait()
     pl.semaphore_wait(barrier, 6)
 
     bufs = (x_buf, dy_buf)
@@ -138,13 +164,13 @@
                     owner = column(k) + a * other1 + b * other2
                     chunk_copy(kind, owner, 1 - c, pe, k * 4 + a * 2 + b, peer).wait_recv()
 
-    def pre(weight, out, n):
+    def pre(core, n, fresh):
         cols = pl.ds(n * TILE, TILE)
-        out[:, cols] = jnp.dot(
-            x_buf[0, :, 0:half], weight[0:half, cols], preferred_element_type=jnp.float32
-        ) + jnp.dot(
-            x_buf[1, :, 0:half], weight[half : 2 * half, cols], preferred_element_type=jnp.float32
-        )
+        depth = pl.ds(pl.multiple_of(core * half, TILE), half)
+        value = jnp.dot(
+            x_buf[core, :, 0:half], wgu[depth, cols], preferred_element_type=jnp.float32
+        )
+        pre_all[:, cols] = value if fresh else pre_all[:, cols] + value
 
     own(0)
     from_part1(0, 0)
@@ -167,22 +193,13 @@
     from_part2(0, 2, 0)
     from_part2(0, 2, 1)
     from_column(1, 2)
+    from_part1(1, 1)
     from_part2(1, 0, 0)
-    from_peer(0)
-    x_copies = [
-        pltpu.make_async_copy(
-            x_buf.at[h, :, 0:half], x_out.at[:, h * half : (h + 1) * half], xo_sem.at[h]
-        )
-        for h in range(2)
-    ]
-    for copy in x_copies:
-        copy.start()
-    work = [(weight, out, n) for weight, out in ((wg, pre_g), (wu, pre_u)) for n in range(hidden // TILE)]
-    rest = [
-        functools.partial(from_part1, 1, 1),
-        functools.partial(from_part2, 1, 0, 1),
+    blocks = 2 * hidden // TILE
+    events = [
         functools.partial(from_part1, 1, 3),
         functools.partial(from_part1, 1, 2),
+        functools.partial(from_part2, 1, 0, 1),
         functools.partial(from_part2, 1, 1, 0),
         functools.partial(from_part2, 1, 1, 1),
         functools.partial(from_part2, 1, 3, 0),
@@ -192,79 +209,129 @@
     ]
     weights[0].wait()
     weights[1].wait()
-    for i, event in enumerate(rest):
+    for n in range(blocks):
+        pre(c, n, True)
+        events[n]()
+    from_peer(0)
+    x_copies = [
+        pltpu.make_async_copy(
+            x_buf.at[h, :, 0:half], x_out.at[:, h * half : (h + 1) * half], xo_sem.at[h]
+        )
+        for h in range(2)
+    ]
+    for copy in x_copies:
+        copy.start()
+    for n in range(blocks):
+        pre(1 - c, n, False)
+        events[blocks + n]()
+    for event in events[2 * blocks :]:
         event()
-        if 0 < i <= len(work):
-            pre(*work[i - 1])
-    for item in work[len(rest) - 1 :]:
-        pre(*item)
     lanes = lax.broadcasted_iota(jnp.int32, (total, LANES), 1)
     scale = jnp.sum(
         jnp.where(lanes == e, x_buf[0, :, half : half + LANES].astype(jnp.float32), 0.0),
         axis=1, keepdims=True,
     )
     weights[2].wait()
+
+    def back(core, n):
+        depth = pl.ds(pl.multiple_of(core * half, TILE), half)
+        return contract_last(dy_buf[core], wd[n * TILE : (n + 1) * TILE, depth])
+
+    own_back = [back(c, n) for n in range(hidden // TILE)]
+    for n, value in enumerate(own_back):
+        back_buf[:, n * TILE : (n + 1) * TILE] = value
     from_peer(1)
     for n in range(hidden // TILE):
         cols = pl.ds(n * TILE, TILE)
-        back = contract_last(dy_buf[0], wd[cols, 0:half]) + contract_last(
-            dy_buf[1], wd[cols, half : 2 * half]
-        )
-        one, two = act_grads(scale, back, pre_g[:, cols], pre_u[:, cols])
-        dg[:, cols] = one
-        du[:, cols] = two
+        upper = pl.ds(hidden + n * TILE, TILE)
+        value = back_buf[:, cols] + back(1 - c, n)
+        one, two = act_grads(scale, value, pre_all[:, cols], pre_all[:, upper])
+        d_all[:, cols] = one
+        d_all[:, upper] = two
 
     def partial(core, n):
         place = pl.ds(pl.multiple_of(core * half + n * TILE, TILE), TILE)
-        return contract_last(dg[...], wg[place, :]) + contract_last(du[...], wu[place, :])
+        return contract_last(d_all[...], wgu[place, :])
+
+    def tile_copy(n):
+        cols = pl.ds(n * TILE, TILE)
+        return remote(part_out.at[:, cols], part_in.at[:, cols], rpe_s.at[n], rpe_r.at[n], peer)
+
+    def other_tiles(span):
+        for n in range(*span):
+            part_out[:, pl.ds(n * TILE, TILE)] = partial(1 - c, n).astype(jnp.bfloat16)
+            go(tile_copy(n))
+
+    def own_tiles(span):
+        for n in range(*span):
+            cols = pl.ds(n * TILE, TILE)
+            mine = partial(c, n)
+            tile_copy(n).wait_recv()
+            acc[:, cols] = (mine + part_in[:, cols].astype(jnp.float32)).astype(jnp.bfloat16)
 
     tiles = half // TILE
-    for n in range(tiles):
-        cols = pl.ds(n * TILE, TILE)
-        part_out[:, cols] = partial(1 - c, n).astype(jnp.bfloat16)
-        go(remote(part_out.at[:, cols], part_in.at[:, cols], rpe_s.at[n], rpe_r.at[n], peer))
-    for n in range(tiles):
-        cols = pl.ds(n * TILE, TILE)
-        mine = partial(c, n)
-        remote(part_out.at[:, cols], part_in.at[:, cols], rpe_s.at[n], rpe_r.at[n], peer).wait_recv()
-        acc[:, cols] = (mine + part_in[:, cols].astype(jnp.float32)).astype(jnp.bfloat16)
-
-    def add(owner, ref):
-        acc[at(owner), :] = (
-            acc[at(owner), :].astype(jnp.float32) + ref[...].astype(jnp.float32)
+    spans = ((0, tiles // 2), (tiles // 2, tiles))
+    order = (2, 1, 3, 0)
+
+    def features(g):
+        return pl.ds(spans[g][0] * TILE, (spans[g][1] - spans[g][0]) * TILE)
+
+    def add(owner, ref, g):
+        cols = features(g)
+        acc[at(owner), cols] = (
+            acc[at(owner), cols].astype(jnp.float32) + ref[:, cols].astype(jnp.float32)
         ).astype(jnp.bfloat16)
 
-    order = (2, 1, 3, 0)
-
-    def second(k, a, owner):
-        idx = k * 2 + a
-        return remote(acc.at[at(owner), :], r2.at[idx], r2_s.at[idx], r2_r.at[idx], part2)
-
-    def first(k, owner):
-        return remote(acc.at[at(owner), :], r1.at[k], r1_s.at[k], r1_r.at[k], part1)
-
-    def third(k, device):
-        return remote(acc.at[at(column(k)), :], rz.at[k - 1], rz_s.at[k - 1], rz_r.at[k - 1], device)
-
-    for k in order:
-        for a in (1, 0):
-            go(second(k, a, column(k) + a * flip1 + flip2))
-    for k in order:
-        for a in (1, 0):
-            second(k, a, column(k) + a * flip1 + flip2).wait_recv()
-            add(column(k) + a * flip1, r2.at[k * 2 + a])
-            if a == 1:
-                go(first(k, column(k) + flip1))
-    for k in order:
-        first(k, column(k) + flip1).wait_recv()
-        add(column(k), r1.at[k])
-        if k:
-            go(third(k, (column(k), c)))
-    result = acc[at(e), :].astype(jnp.float32)
-    for k in (1, 2, 3):
-        third(k, (column(k), c)).wait_recv()
-        result += rz[k - 1].astype(jnp.float32)
-    gt_out[...] = result.astype(jnp.bfloat16)
+    def hop(owner, slots, i, sems, g, device):
+        cols = features(g)
+        return remote(
+            acc.at[at(owner), cols], slots.at[i, :, cols], sems[0].at[g, i], sems[1].at[g, i], device
+        )
+
+    def second(k, a, g):
+        return hop(column(k) + a * flip1 + flip2, r2, k * 2 + a, (r2_s, r2_r), g, part2)
+
+    def first(k, g):
+        return hop(column(k) + flip1, r1, k, (r1_s, r1_r), g, part1)
+
+    def third(k, g):
+        return hop(column(k), rz, k - 1, (rz_s, rz_r), g, (column(k), c))
+
+    def send_second(g):
+        for k in order:
+            for a in (1, 0):
+                go(second(k, a, g))
+
+    def send_first(g):
+        for k in order:
+            for a in (1, 0):
+                second(k, a, g).wait_recv()
+                add(column(k) + a * flip1, r2.at[k * 2 + a], g)
+                if a == 1:
+                    go(first(k, g))
+
+    def send_third(g):
+        for k in order:
+            first(k, g).wait_recv()
+            add(column(k), r1.at[k], g)
+            if k:
+                go(third(k, g))
+
+    def finish(g):
+        cols = features(g)
+        result = acc[at(e), cols].astype(jnp.float32)
+        for k in (1, 3, 2):
+            third(k, g).wait_recv()
+            result += rz[k - 1, :, cols].astype(jnp.float32)
+        gt_out[:, cols] = result.astype(jnp.bfloat16)
+
+    for g in range(2):
+        other_tiles(spans[g])
+        own_tiles(spans[g])
+        send_second(g)
+    for stage in (send_first, send_third, finish):
+        for g in range(2):
+            stage(g)
     for copy in x_copies:
         copy.wait()
     for copy in sent:
@@ -281,23 +348,21 @@
     bf16 = jnp.bfloat16
     dma = pltpu.SemaphoreType.DMA
     tiles = half // TILE
-    grad_tokens, rows_x, d_gate, d_up = pl.pallas_call(
+    grad_tokens, rows_x, d_all = pl.pallas_call(
         kernel,
         out_shape=(
             jax.ShapeDtypeStruct((rows, half), bf16),
             jax.ShapeDtypeStruct((total, width), bf16),
-            jax.ShapeDtypeStruct((total, hidden), bf16),
-            jax.ShapeDtypeStruct((total, hidden), bf16),
+            jax.ShapeDtypeStruct((total, 2 * hidden), bf16),
         ),
-        in_specs=[vmem] * 4 + [hbm] * 3,
-        out_specs=(vmem, hbm, vmem, vmem),
+        in_specs=[hbm] * 2 + [vmem] * 2 + [hbm] * 3,
+        out_specs=(vmem, hbm, vmem),
         scratch_shapes=[
             pltpu.VMEM((2, total, half + LANES), bf16),
             pltpu.VMEM((2, total, half), bf16),
-            pltpu.VMEM((width, hidden), bf16),
-            pltpu.VMEM((width, hidden), bf16),
+            pltpu.VMEM((width, 2 * hidden), bf16),
             pltpu.VMEM((hidden, width), bf16),
-            pltpu.VMEM((total, hidden), jnp.float32),
+            pltpu.VMEM((total, 2 * hidden), jnp.float32),
             pltpu.VMEM((total, hidden), jnp.float32),
             pltpu.VMEM((total, half), bf16),
             pltpu.VMEM((total, half), bf16),
@@ -305,11 +370,11 @@
             pltpu.VMEM((8, rows, half), bf16),
             pltpu.VMEM((4, rows, half), bf16),
             pltpu.VMEM((3, rows, half), bf16),
-            dma((3,)), dma((2,)),
+            dma((2,)), dma((3,)), dma((2,)),
             dma((2, 3)), dma((2, 3)), dma((2, 4)), dma((2, 4)),
             dma((2, 8)), dma((2, 8)), dma((2, 16)), dma((2, 16)),
-            dma((tiles,)), dma((tiles,)), dma((8,)), dma((8,)),
-            dma((4,)), dma((4,)), dma((3,)), dma((3,)),
+            dma((tiles,)), dma((tiles,)), dma((2, 8)), dma((2, 8)),
+            dma((2, 4)), dma((2, 4)), dma((2, 3)), dma((2, 3)),
         ],
         compiler_params=pltpu.CompilerParams(
             collective_id=0, has_side_effects=True, vmem_limit_bytes=60 << 20
@@ -318,9 +383,27 @@
             flops=10 * total * width * hidden, bytes_accessed=6 * width * hidden, transcendentals=0
         ),
         name="gather_grads_scatter",
-    )(tokens, grad_out, gate_weights, routing, w_gate[0], w_up[0], w_down[0])
-    grad_g = contract_first(rows_x, d_gate).astype(bf16)[None]
-    grad_u = contract_first(rows_x, d_up).astype(bf16)[None]
+    )(tokens, grad_out, gate_weights.T, routing.T, w_gate[0], w_up[0], w_down[0])
+    block = 2 * TILE
+    grads = jax.ShapeDtypeStruct((1, width, hidden), bf16)
+    grad_g, grad_u = pl.pallas_call(
+        weight_grads,
+        grid=(width // block,),
+        out_shape=(grads, grads),
+        in_specs=[
+            pl.BlockSpec((total, block), lambda i: (0, i)),
+            pl.BlockSpec((total, 2 * hidden), lambda i: (0, 0)),
+        ],
+        out_specs=(
+            pl.BlockSpec((1, block, hidden), lambda i: (0, i, 0)),
+            pl.BlockSpec((1, block, hidden), lambda i: (0, i, 0)),
+        ),
+        compiler_params=pltpu.CompilerParams(vmem_limit_bytes=60 << 20),
+        cost_estimate=pl.CostEstimate(
+            flops=4 * total * width * hidden, bytes_accessed=4 * width * hidden, transcendentals=0
+        ),
+        name="weight_grads",
+    )(rows_x, d_all)
     return (grad_tokens, grad_g, grad_u)
 
 

time: 67 us -> 63.5 us (0.948)
  matrix products: 7.62 us -> 0 us
  Pallas kernels: 55.2 us -> 61.9 us
  local copies, waits for them, and re-layouts: 3.34 us -> 0.63 us
    dot_general x2 -> x0, matrix products: 7.62 us -> none  [contract_first(): lax.dot_general(left, right, (((0,), (0,)), ((), ())), preferred_element_...]
    pallas_call x0 -> x1, Pallas kernels: none -> 7.32 us  [fused(): pl.pallas_call(weight_grads, grid=(width // block,), out_shape=(grads, gr...]
    unnamed x9 -> x3, local copies, waits for them, and re-layouts: 3.34 us -> 0.63 us
where the time goes in v2:
time: 63.5 us; the launch traced here: 63.2 us
  Pallas kernels  61.9 us (97%)
  between operations  0.65 us (1%)
    pallas_call x1, Pallas kernels, fused(): pl.pallas_call(kernel, out_shape=(jax.ShapeDtypeStruct((rows, half), bf16...  54.6 us
    pallas_call x1, Pallas kernels, fused(): pl.pallas_call(weight_grads, grid=(width // block,), out_shape=(grads, gr...  7.32 us

profile of v2, /device:TPU:0, one launch (start us, length us, event | category | flops | bytes accessed | tf_op | source)
XLA Modules:
  0.0 63.2 jit_solution(6813206377726251276)
XLA Ops:
  0.6 54.6 %gather_grads_scatter.1 = (bf16[16,1792]{1,0:T(8,128)(2,1)}, bf16[256,3584]{1,0:T(8,128)(2,1)}, bf16[256,1024]{1,0:T(8,128)(2,1)}) custom-call(bf16[16,1792]{1,0:T(8,128)(2,1)} %tok.1, bf16[16,1792]{1,0:T(8,128)(2,1)} %gro.1, bf16[8,16]{1,0:T(8,128)(2,1)} %bitcast.9, s32[8,16]{1,0:T(8,128)} %bitcast.8, bf16[3584,512]{1,0:T(8,128)(2,1)} %bitcast.5, ...), custom_call_target="tpu_custom_call" | custom-call | flops 4697620480 | bytes 11010048 | tf_op jit(solution)/shard_map/gather_grads_scatter/pallas_call | solution.py:351
  55.3 0.0 copy-start
  55.3 7.3 %weight_grads.1 = (bf16[1,3584,512]{2,1,0:T(8,128)(2,1)}, bf16[1,3584,512]{2,1,0:T(8,128)(2,1)}) custom-call(bf16[256,3584]{1,0:T(8,128)(2,1)} %get-tuple-element.9.x_ref, bf16[256,1024]{1,0:T(8,128)(2,1)} %get-tuple-element.10.d_ref), custom_call_target="tpu_custom_call" | custom-call | flops 1879048192 | bytes 7340032 | tf_op jit(solution)/shard_map/weight_grads/pallas_call | solution.py:389
  62.6 0.0 copy-done
  62.6 0.6 copy.11
Async XLA Ops:
  55.3 7.3 %copy-start = (bf16[16,1792]{1,0:T(8,128)(2,1)S(1)}, bf16[16,1792]{1,0:T(8,128)(2,1)}, u32[]{:S(2)}) copy-start(bf16[16,1792]{1,0:T(8,128)(2,1)} %get-tuple-element.16) | copy-start | bytes 172036

commit v3 on v2

--- a/solution.py
+++ b/solution.py
@@ -29,18 +29,11 @@
     return d_gate.astype(jnp.bfloat16), d_up.astype(jnp.bfloat16)
 
 
-def weight_grads(x_ref, d_ref, gate_ref, up_ref):
-    hidden = gate_ref.shape[2]
-    both = contract_first(x_ref[...], d_ref[...]).astype(jnp.bfloat16)
-    gate_ref[0] = both[:, 0:hidden]
-    up_ref[0] = both[:, hidden : 2 * hidden]
-
-
 def kernel(
     tok, gro, gw, rt, wg_hbm, wu_hbm, wd_hbm,
-    gt_out, x_out, d_all,
-    x_buf, dy_buf, wgu, wd, pre_all, back_buf, part_out, part_in, acc, r2, r1, rz,
-    in_sem, w_sem, xo_sem, z_s, z_r, p1_s, p1_r, p2_s, p2_r, pe_s, pe_r,
+    gt_out, gate_out, up_out,
+    x_buf, dy_buf, d_all, wgu, wd, pre_all, back_buf, part_out, part_in, acc, r2, r1, rz,
+    in_sem, w_sem, z_s, z_r, p1_s, p1_r, p2_s, p2_r, pe_s, pe_r,
     rpe_s, rpe_r, r2_s, r2_r, r1_s, r1_r, rz_s, rz_r,
 ):
     e = lax.axis_index("expert")
@@ -213,14 +206,6 @@
         pre(c, n, True)
         events[n]()
     from_peer(0)
-    x_copies = [
-        pltpu.make_async_copy(
-            x_buf.at[h, :, 0:half], x_out.at[:, h * half : (h + 1) * half], xo_sem.at[h]
-        )
-        for h in range(2)
-    ]
-    for copy in x_copies:
-        copy.start()
     for n in range(blocks):
         pre(1 - c, n, False)
         events[blocks + n]()
@@ -329,11 +314,26 @@
         other_tiles(spans[g])
         own_tiles(spans[g])
         send_second(g)
-    for stage in (send_first, send_third, finish):
-        for g in range(2):
-            stage(g)
-    for copy in x_copies:
-        copy.wait()
+    def weight_grads(first_tile, last_tile):
+        for n in range(first_tile, last_tile):
+            core, inner = n // tiles, n % tiles
+            both = contract_first(
+                x_buf[core, :, inner * TILE : (inner + 1) * TILE], d_all[...]
+            ).astype(jnp.bfloat16)
+            gate_out[0, n * TILE : (n + 1) * TILE, :] = both[:, 0:hidden]
+            up_out[0, n * TILE : (n + 1) * TILE, :] = both[:, hidden : 2 * hidden]
+
+    quarter = 2 * tiles // 4
+    send_first(0)
+    weight_grads(0, quarter)
+    send_first(1)
+    weight_grads(quarter, 2 * quarter)
+    send_third(0)
+    weight_grads(2 * quarter, 3 * quarter)
+    send_third(1)
+    weight_grads(3 * quarter, 2 * tiles)
+    finish(0)
+    finish(1)
     for copy in sent:
         copy.wait_send()
 
@@ -344,22 +344,24 @@
     total = experts * rows
     width, hidden = w_gate.shape[1:]
     vmem = pl.BlockSpec(memory_space=pltpu.VMEM)
-    hbm = pl.BlockSpec(memory_space=pl.ANY)
+    hbm = pl.BlockSpec(memory_space=pltpu.HBM)
     bf16 = jnp.bfloat16
     dma = pltpu.SemaphoreType.DMA
     tiles = half // TILE
-    grad_tokens, rows_x, d_all = pl.pallas_call(
+    grads = jax.ShapeDtypeStruct((1, width, hidden), bf16)
+    return pl.pallas_call(
         kernel,
         out_shape=(
             jax.ShapeDtypeStruct((rows, half), bf16),
-            jax.ShapeDtypeStruct((total, width), bf16),
-            jax.ShapeDtypeStruct((total, 2 * hidden), bf16),
+            grads,
+            grads,
         ),
         in_specs=[hbm] * 2 + [vmem] * 2 + [hbm] * 3,
-        out_specs=(vmem, hbm, vmem),
+        out_specs=(vmem, vmem, vmem),
         scratch_shapes=[
             pltpu.VMEM((2, total, half + LANES), bf16),
             pltpu.VMEM((2, total, half), bf16),
+            pltpu.VMEM((total, 2 * hidden), bf16),
             pltpu.VMEM((width, 2 * hidden), bf16),
             pltpu.VMEM((hidden, width), bf16),
             pltpu.VMEM((total, 2 * hidden), jnp.float32),
@@ -370,41 +372,20 @@
             pltpu.VMEM((8, rows, half), bf16),
             pltpu.VMEM((4, rows, half), bf16),
             pltpu.VMEM((3, rows, half), bf16),
-            dma((2,)), dma((3,)), dma((2,)),
+            dma((2,)), dma((3,)),
             dma((2, 3)), dma((2, 3)), dma((2, 4)), dma((2, 4)),
             dma((2, 8)), dma((2, 8)), dma((2, 16)), dma((2, 16)),
             dma((tiles,)), dma((tiles,)), dma((2, 8)), dma((2, 8)),
             dma((2, 4)), dma((2, 4)), dma((2, 3)), dma((2, 3)),
         ],
         compiler_params=pltpu.CompilerParams(
-            collective_id=0, has_side_effects=True, vmem_limit_bytes=60 << 20
+            collective_id=0, has_side_effects=True, vmem_limit_bytes=45 << 20
         ),
         cost_estimate=pl.CostEstimate(
-            flops=10 * total * width * hidden, bytes_accessed=6 * width * hidden, transcendentals=0
+            flops=14 * total * width * hidden, bytes_accessed=6 * width * hidden, transcendentals=0
         ),
         name="gather_grads_scatter",
     )(tokens, grad_out, gate_weights.T, routing.T, w_gate[0], w_up[0], w_down[0])
-    block = 2 * TILE
-    grads = jax.ShapeDtypeStruct((1, width, hidden), bf16)
-    grad_g, grad_u = pl.pallas_call(
-        weight_grads,
-        grid=(width // block,),
-        out_shape=(grads, grads),
-        in_specs=[
-            pl.BlockSpec((total, block), lambda i: (0, i)),
-            pl.BlockSpec((total, 2 * hidden), lambda i: (0, 0)),
-        ],
-        out_specs=(
-            pl.BlockSpec((1, block, hidden), lambda i: (0, i, 0)),
-            pl.BlockSpec((1, block, hidden), lambda i: (0, i, 0)),
-        ),
-        compiler_params=pltpu.CompilerParams(vmem_limit_bytes=60 << 20),
-        cost_estimate=pl.CostEstimate(
-            flops=4 * total * width * hidden, bytes_accessed=4 * width * hidden, transcendentals=0
-        ),
-        name="weight_grads",
-    )(rows_x, d_all)
-    return (grad_tokens, grad_g, grad_u)
 
 
 def dense(tokens, grad_out, gate_weights, routing, w_gate, w_up, w_down):

time: 63.5 us -> 61.1 us (0.962)
  Pallas kernels: 61.9 us -> 52.8 us
  local copies, waits for them, and re-layouts: 0.63 us -> 7.29 us
    pallas_call x1 -> x0, Pallas kernels: 7.32 us -> none  [fused(): pl.pallas_call(weight_grads, grid=(width // block,), out_shape=(grads, gr...]
    unnamed x3 -> x11, local copies, waits for them, and re-layouts: 0.63 us -> 7.29 us
    pallas_call x1, Pallas kernels: 54.6 us -> 52.8 us  [fused(): pl.pallas_call(kernel, out_shape=(jax.ShapeDtypeStruct((rows, half), bf16...]
where the time goes in v3:
time: 61.1 us; the launch traced here: 60.8 us
  Pallas kernels  52.8 us (86%)
  local copies, waits for them, and re-layouts  7.29 us (12%)
  between operations  0.65 us (1%)
    pallas_call x1, Pallas kernels, fused(): pl.pallas_call(kernel, out_shape=(jax.ShapeDtypeStruct((rows, half), bf16...  52.8 us
    unnamed x11, local copies, waits for them, and re-layouts  7.29 us

profile of v3, /device:TPU:0, one launch (start us, length us, event | category | flops | bytes accessed | tf_op | source)
XLA Modules:
  0.0 60.8 jit_solution(9759039698150626232)
XLA Ops:
  0.6 0.0 copy-start
  0.6 0.8 %copy-done = bf16[16,1792]{1,0:T(8,128)(2,1)S(1)} copy-done((bf16[16,1792]{1,0:T(8,128)(2,1)S(1)}, bf16[16,1792]{1,0:T(8,128)(2,1)}, u32[]{:S(2)}) %copy-start) | copy-done | bytes 57368
  1.5 0.0 copy-start.1
  1.5 0.8 %copy-done.1 = bf16[16,1792]{1,0:T(8,128)(2,1)S(1)} copy-done((bf16[16,1792]{1,0:T(8,128)(2,1)S(1)}, bf16[16,1792]{1,0:T(8,128)(2,1)}, u32[]{:S(2)}) %copy-start.1) | copy-done | bytes 57368
  2.3 0.0 copy-start.2
  2.3 0.7 %copy-done.2 = s32[16,8]{0,1:T(8,128)S(1)} copy-done((s32[16,8]{0,1:T(8,128)S(1)}, s32[16,8]{0,1:T(8,128)}, u32[]{:S(2)}) %copy-start.2) | copy-done | bytes 536
  3.0 0.0 copy-start.3
  3.0 0.7 %copy-done.3 = bf16[16,8]{0,1:T(8,128)(2,1)S(1)} copy-done((bf16[16,8]{0,1:T(8,128)(2,1)S(1)}, bf16[16,8]{0,1:T(8,128)(2,1)}, u32[]{:S(2)}) %copy-start.3) | copy-done | bytes 280
  3.6 52.8 %gather_grads_scatter.1 = (bf16[16,1792]{1,0:T(8,128)(2,1)S(1)}, bf16[1,3584,512]{2,1,0:T(8,128)(2,1)S(1)}, bf16[1,3584,512]{2,1,0:T(8,128)(2,1)S(1)}) custom-call(bf16[16,1792]{1,0:T(8,128)(2,1)S(1)} %copy-done, bf16[16,1792]{1,0:T(8,128)(2,1)S(1)} %copy-done.1, bf16[8,16]{1,0:T(8,128)(2,1)S(1)} %bitcast.6, s32[8,16]{1,0:T(8,128)S(1)} %bitcast.5, ...), custom_call_target="tpu_custom_call" | custom-call | flops 6576668672 | bytes 11010048 | tf_op jit(solution)/shard_map/gather_grads_scatter/pallas_call | solution.py:352
  56.5 0.6 %copy.13 = bf16[16,1792]{1,0:T(8,128)(2,1)} copy(bf16[16,1792]{1,0:T(8,128)(2,1)S(1)} %get-tuple-element.6) | data formatting | bytes 114688
  57.1 1.8 %copy.14 = bf16[1,3584,512]{2,1,0:T(8,128)(2,1)} copy(bf16[1,3584,512]{2,1,0:T(8,128)(2,1)S(1)} %get-tuple-element.7) | data formatting | bytes 7340032
  59.0 1.8 %copy.15 = bf16[1,3584,512]{2,1,0:T(8,128)(2,1)} copy(bf16[1,3584,512]{2,1,0:T(8,128)(2,1)S(1)} %get-tuple-element.8) | data formatting | bytes 7340032
Async XLA Ops:
  0.6 0.8 %copy-start = (bf16[16,1792]{1,0:T(8,128)(2,1)S(1)}, bf16[16,1792]{1,0:T(8,128)(2,1)}, u32[]{:S(2)}) copy-start(bf16[16,1792]{1,0:T(8,128)(2,1)} %tok.1) | copy-start | bytes 172036
  1.5 0.8 %copy-start.1 = (bf16[16,1792]{1,0:T(8,128)(2,1)S(1)}, bf16[16,1792]{1,0:T(8,128)(2,1)}, u32[]{:S(2)}) copy-start(bf16[16,1792]{1,0:T(8,128)(2,1)} %gro.1) | copy-start | bytes 172036
  2.3 0.7 %copy-start.2 = (s32[16,8]{0,1:T(8,128)S(1)}, s32[16,8]{0,1:T(8,128)}, u32[]{:S(2)}) copy-start(s32[16,8]{0,1:T(8,128)} %param.10) | copy-start | bytes 1540
  3.0 0.7 %copy-start.3 = (bf16[16,8]{0,1:T(8,128)(2,1)S(1)}, bf16[16,8]{0,1:T(8,128)(2,1)}, u32[]{:S(2)}) copy-start(bf16[16,8]{0,1:T(8,128)(2,1)} %param.9) | copy-start | bytes 772

commit v4 on v3

--- a/solution.py
+++ b/solution.py
@@ -127,9 +127,11 @@
     def to_part1(kind, k):
         go(chunk_copy(kind, column(k), c, p1, k, part1))
 
-    def own(kind):
+    def own_column(kind):
         for k in (2, 1, 3):
             go(chunk_copy(kind, e, c, zs, k - 1, (column(k), c)))
+
+    def own(kind):
         to_part1(kind, 0)
         to_part2(kind, 0, 0)
         to_peer(kind, 0, 0, 0)
@@ -165,8 +167,10 @@
         )
         pre_all[:, cols] = value if fresh else pre_all[:, cols] + value
 
+    own_column(0)
     own(0)
     from_part1(0, 0)
+    own_column(1)
     from_column(0, 1)
     from_column(0, 3)
     from_part2(0, 0, 0)

time: 61.1 us -> 62.5 us (1.023)
  Pallas kernels: 52.8 us -> 54.3 us
    pallas_call x1, Pallas kernels: 52.8 us -> 54.3 us  [fused(): pl.pallas_call(kernel, out_shape=(jax.ShapeDtypeStruct((rows, half), bf16...]
where the time goes in v4:
time: 62.5 us; the launch traced here: 62.2 us
  Pallas kernels  54.3 us (87%)
  local copies, waits for them, and re-layouts  7.29 us (12%)
  between operations  0.65 us (1%)
    pallas_call x1, Pallas kernels, fused(): pl.pallas_call(kernel, out_shape=(jax.ShapeDtypeStruct((rows, half), bf16...  54.3 us
    unnamed x11, local copies, waits for them, and re-layouts  7.29 us

profile of v4, /device:TPU:0, one launch (start us, length us, event | category | flops | bytes accessed | tf_op | source)
XLA Modules:
  0.0 62.2 jit_solution(2574881785891849257)
XLA Ops:
  0.6 0.0 copy-start
  0.6 0.8 %copy-done = bf16[16,1792]{1,0:T(8,128)(2,1)S(1)} copy-done((bf16[16,1792]{1,0:T(8,128)(2,1)S(1)}, bf16[16,1792]{1,0:T(8,128)(2,1)}, u32[]{:S(2)}) %copy-start) | copy-done | bytes 57368
  1.5 0.0 copy-start.1
  1.5 0.8 %copy-done.1 = bf16[16,1792]{1,0:T(8,128)(2,1)S(1)} copy-done((bf16[16,1792]{1,0:T(8,128)(2,1)S(1)}, bf16[16,1792]{1,0:T(8,128)(2,1)}, u32[]{:S(2)}) %copy-start.1) | copy-done | bytes 57368
  2.3 0.0 copy-start.2
  2.3 0.7 %copy-done.2 = s32[16,8]{0,1:T(8,128)S(1)} copy-done((s32[16,8]{0,1:T(8,128)S(1)}, s32[16,8]{0,1:T(8,128)}, u32[]{:S(2)}) %copy-start.2) | copy-done | bytes 536
  3.0 0.0 copy-start.3
  3.0 0.7 %copy-done.3 = bf16[16,8]{0,1:T(8,128)(2,1)S(1)} copy-done((bf16[16,8]{0,1:T(8,128)(2,1)S(1)}, bf16[16,8]{0,1:T(8,128)(2,1)}, u32[]{:S(2)}) %copy-start.3) | copy-done | bytes 280
  3.6 54.3 %gather_grads_scatter.1 = (bf16[16,1792]{1,0:T(8,128)(2,1)S(1)}, bf16[1,3584,512]{2,1,0:T(8,128)(2,1)S(1)}, bf16[1,3584,512]{2,1,0:T(8,128)(2,1)S(1)}) custom-call(bf16[16,1792]{1,0:T(8,128)(2,1)S(1)} %copy-done, bf16[16,1792]{1,0:T(8,128)(2,1)S(1)} %copy-done.1, bf16[8,16]{1,0:T(8,128)(2,1)S(1)} %bitcast.6, s32[8,16]{1,0:T(8,128)S(1)} %bitcast.5, ...), custom_call_target="tpu_custom_call" | custom-call | flops 6576668672 | bytes 11010048 | tf_op jit(solution)/shard_map/gather_grads_scatter/pallas_call | solution.py:356
  57.9 0.6 %copy.13 = bf16[16,1792]{1,0:T(8,128)(2,1)} copy(bf16[16,1792]{1,0:T(8,128)(2,1)S(1)} %get-tuple-element.6) | data formatting | bytes 114688
  58.6 1.8 %copy.14 = bf16[1,3584,512]{2,1,0:T(8,128)(2,1)} copy(bf16[1,3584,512]{2,1,0:T(8,128)(2,1)S(1)} %get-tuple-element.7) | data formatting | bytes 7340032
  60.4 1.8 %copy.15 = bf16[1,3584,512]{2,1,0:T(8,128)(2,1)} copy(bf16[1,3584,512]{2,1,0:T(8,128)(2,1)S(1)} %get-tuple-element.8) | data formatting | bytes 7340032
Async XLA Ops:
  0.6 0.8 %copy-start = (bf16[16,1792]{1,0:T(8,128)(2,1)S(1)}, bf16[16,1792]{1,0:T(8,128)(2,1)}, u32[]{:S(2)}) copy-start(bf16[16,1792]{1,0:T(8,128)(2,1)} %tok.1) | copy-start | bytes 172036
  1.5 0.8 %copy-start.1 = (bf16[16,1792]{1,0:T(8,128)(2,1)S(1)}, bf16[16,1792]{1,0:T(8,128)(2,1)}, u32[]{:S(2)}) copy-start(bf16[16,1792]{1,0:T(8,128)(2,1)} %gro.1) | copy-start | bytes 172036
  2.3 0.7 %copy-start.2 = (s32[16,8]{0,1:T(8,128)S(1)}, s32[16,8]{0,1:T(8,128)}, u32[]{:S(2)}) copy-start(s32[16,8]{0,1:T(8,128)} %param.10) | copy-start | bytes 1540
  3.0 0.7 %copy-start.3 = (bf16[16,8]{0,1:T(8,128)(2,1)S(1)}, bf16[16,8]{0,1:T(8,128)(2,1)}, u32[]{:S(2)}) copy-start(bf16[16,8]{0,1:T(8,128)(2,1)} %param.9) | copy-start | bytes 772
